TPU v7x, 32 devices: a whole 2x2x4 slice. The times are simulated.
32 devices in a mesh: items: 2 (over y), codes: 16 (over z, x, core).
Axes of the slice: x: 2, y: 2, z: 4, core: 2. Of those that a mesh axis runs over, the one named last changes fastest.
Arguments:
- residuals: bfloat16 [512, 256], P(('items', 'codes')), may hold values from -6 to 6
- codebook: bfloat16 [4096, 256], P('codes'), may hold values from -6 to 6
Outputs:
- new_codebook: float32 [4096, 256], P('codes')
- next_residuals: float32 [512, 256], P(('items', 'codes'))
All inputs are finite; a program needn't handle non-finite values.
Results may differ from a plain program's by a relative error of at most 0.0024.
Values may be sent and summed in bfloat16 or wider, within the bound.
A program may use at most 64 MiB of HBM per device.

v0:
```python
import jax
import jax.numpy as jnp
from jax import lax
from jax.sharding import PartitionSpec as P

ITERS = 3


EPSILON = 1e-06
SHARPNESS = 40.0


def shards(residuals, codebook):
    gathered = lax.all_gather(residuals, "codes", axis=0, tiled=True)
    feature_count = gathered.shape[1]
    rows_float = gathered.astype(jnp.float32)
    codes_float = codebook.astype(jnp.float32)
    row_scale = lax.rsqrt(jnp.mean(rows_float * rows_float, axis=1) + EPSILON)
    code_scale = lax.rsqrt(jnp.mean(codes_float * codes_float, axis=1) + EPSILON)
    similarity = lax.dot_general(
        gathered, codebook, (((1,), (1,)), ((), ())), preferred_element_type=jnp.float32
    )
    kernel = jnp.exp(
        SHARPNESS * similarity * row_scale[:, None] * code_scale[None, :] / feature_count
    )
    balance = gathered.shape[0] * lax.axis_size("items") / codebook.shape[0]
    weights_rows = jnp.ones((gathered.shape[0],), jnp.float32)
    weights_cols = jnp.ones((codebook.shape[0],), jnp.float32)
    for sweep in range(ITERS):
        column_total = lax.psum(
            jnp.dot(weights_rows, kernel, precision=lax.Precision.HIGHEST), "items"
        )
        weights_cols = balance / column_total
        row_total = lax.psum(
            jnp.dot(kernel, weights_cols, precision=lax.Precision.HIGHEST), "codes"
        )
        weights_rows = 1.0 / row_total
    transport = (kernel * weights_rows[:, None] * weights_cols[None, :]).astype(jnp.bfloat16)
    numerator = lax.dot_general(
        transport, gathered, (((0,), (0,)), ((), ())), preferred_element_type=jnp.float32
    )
    mass = jnp.sum(transport.astype(jnp.float32), axis=0)
    numerator, mass = lax.psum((numerator, mass), "items")
    new_codebook = numerator / mass[:, None]
    moved = lax.all_to_all(transport, "codes", split_axis=0, concat_axis=1, tiled=True)
    rebuilt = jnp.dot(
        moved,
        lax.all_gather(codebook, "codes", axis=0, tiled=True),
        preferred_element_type=jnp.float32,
    )
    following = residuals.astype(jnp.float32) - rebuilt
    return (new_codebook, following)


def solution(mesh):
    return jax.shard_map(
        shards,
        mesh=mesh,
        in_specs=(P(("items", "codes"), None), P("codes", None)),
        out_specs=(P("codes", None), P(("items", "codes"), None)),
        check_vma=False,
    )
```

profile of v0, /device:TPU:0, one launch (start us, length us, event | category | flops | bytes accessed | tf_op | source)
XLA Modules:
  0.0 193.4 jit_solution(1141660528239931592)
XLA Ops:
  8.0 0.0 all-reduce.2.cloned.1.call-start
  8.0 23.7 %all_gather.6 = bf16[256,256]{1,0:T(8,128)(2,1)S(1)} all-gather(bf16[16,256]{1,0:T(8,128)(2,1)} %param.2), channel_id=1, replica_groups=mesh['items'=2,'codes'=16] {'codes'}, dimensions={0}, use_global_device_ids=true | all-gather | bytes 139264 | tf_op jit(solution)/shard_map/all_gather | solution.py:14
  31.7 0.1 multiply_reduce_fusion.1
  31.8 1.0 multiply_reduce_fusion
  32.9 1.1 fusion.2
  34.0 0.0 copy-start
  34.0 0.2 fusion.3
  34.2 5.0 %psum.56 = f32[256]{0:T(256)S(1)} all-reduce(f32[256]{0:T(256)S(1)} %bitcast.43), channel_id=1, replica_groups=mesh['items'=2,'codes'=16] {'items'}, use_global_device_ids=true, to_apply=%region_2.0 | all-reduce | flops 256 | bytes 2048 | tf_op jit(solution)/shard_map/psum | solution.py:30
  39.2 0.3 fusion.6
  39.5 29.5 %psum.57 = f32[256]{0:T(256)S(1)} all-reduce(f32[256]{0:T(256)S(1)} %bitcast.36), channel_id=1, replica_groups=mesh['items'=2,'codes'=16] {'codes'}, use_global_device_ids=true, to_apply=%region_3.0 | all-reduce | flops 256 | bytes 2048 | tf_op jit(solution)/shard_map/psum | solution.py:34
  69.0 0.2 fusion.7
  69.2 5.0 %psum.58 = f32[256]{0:T(256)S(1)} all-reduce(f32[256]{0:T(256)S(1)} %bitcast.38), channel_id=1, replica_groups=mesh['items'=2,'codes'=16] {'items'}, use_global_device_ids=true, to_apply=%region_4.0 | all-reduce | flops 256 | bytes 2048 | tf_op jit(solution)/shard_map/psum | solution.py:30
  74.2 0.3 fusion.8
  74.4 29.5 %psum.59 = f32[256]{0:T(256)S(1)} all-reduce(f32[256]{0:T(256)S(1)} %bitcast.40), channel_id=1, replica_groups=mesh['items'=2,'codes'=16] {'codes'}, use_global_device_ids=true, to_apply=%region_5.0 | all-reduce | flops 256 | bytes 2048 | tf_op jit(solution)/shard_map/psum | solution.py:34
  104.0 0.2 fusion.9
  104.2 5.0 %psum.60 = f32[256]{0:T(256)S(1)} all-reduce(f32[256]{0:T(256)S(1)} %bitcast.42), channel_id=1, replica_groups=mesh['items'=2,'codes'=16] {'items'}, use_global_device_ids=true, to_apply=%region_6.0 | all-reduce | flops 256 | bytes 2048 | tf_op jit(solution)/shard_map/psum | solution.py:30
  109.1 0.3 fusion.10
  109.4 29.5 %psum.61 = f32[256]{0:T(256)S(1)} all-reduce(f32[256]{0:T(256)S(1)} %bitcast.44), channel_id=1, replica_groups=mesh['items'=2,'codes'=16] {'codes'}, use_global_device_ids=true, to_apply=%region_7.0 | all-reduce | flops 256 | bytes 2048 | tf_op jit(solution)/shard_map/psum | solution.py:34
  139.0 0.8 convert_reduce_fusion
  139.7 1.8 fusion.11
  141.5 0.0 all-reduce.2.cloned.1.call-update
  141.6 0.0 all-gather.2.cloned.1.call-start
  141.6 0.5 all-gather.2.cloned.1.call-update
  142.2 3.5 %all-to-all-start = ((bf16[16,16,256]{2,1,0:T(8,128)(2,1)}), bf16[16,16,256]{2,1,0:T(8,128)(2,1)S(1)}, u32[]{:S(2)}, u32[]{:S(2)}) async-start(bf16[16,16,256]{2,1,0:T(8,128)(2,1)} %bitcast.11), calls=%async_computation | async-start | bytes 262144 | tf_op jit(solution)/shard_map/all_to_all | solution.py:45
  145.7 4.9 %psum.63 = f32[256]{0:T(256)S(1)} all-reduce(f32[256]{0:T(256)S(1)} %get-tuple-element.2), channel_id=1, replica_groups=mesh['items'=2,'codes'=16] {'items'}, use_global_device_ids=true, to_apply=%region_10.0 | all-reduce | flops 256 | bytes 2048 | tf_op jit(solution)/shard_map/psum | solution.py:43
  150.6 3.1 %all-to-all-done = bf16[16,16,256]{2,1,0:T(8,128)(2,1)S(1)} async-done(((bf16[16,16,256]{2,1,0:T(8,128)(2,1)}), bf16[16,16,256]{2,1,0:T(8,128)(2,1)S(1)}, u32[]{:S(2)}, u32[]{:S(2)}) %all-to-all-start) | async-done | bytes 131104 | tf_op jit(solution)/shard_map/all_to_all | solution.py:45
  153.7 8.6 %all-reduce.2.cloned.1.call-done = f32[256,256]{1,0:T(8,128)} async-done(((f32[256,256]{1,0:T(8,128)}), f32[256,256]{1,0:T(8,128)}) %all-reduce.2.cloned.1.call-update) | async-done | bytes 262160 | tf_op jit(solution)/shard_map/psum | solution.py:43
  162.3 1.8 broadcast_divide_fusion
  164.0 19.3 %all-gather.2.cloned.1.call-done = bf16[4096,256]{1,0:T(8,128)(2,1)} async-done(((bf16[256,256]{1,0:T(8,128)(2,1)}), bf16[4096,256]{1,0:T(8,128)(2,1)}) %all-gather.2.cloned.1.call-update) | async-done | bytes 2097168 | tf_op jit(solution)/shard_map/all_gather | solution.py:48
  183.3 0.0 copy-done
  183.3 2.6 %convolution_subtract_fusion = f32[16,256]{1,0:T(8,128)} fusion(bf16[16,4096]{1,0:T(8,128)(2,1)S(1)} %bitcast.32, bf16[4096,256]{1,0:T(8,128)(2,1)} %all-gather.2.cloned.1.call-done, bf16[16,256]{1,0:T(8,128)(2,1)S(1)} %copy-done), kind=kOutput, calls=%fused_computation.4 | convolution fusion | flops 33562624 | bytes 2252800 | tf_op jit(solution)/shard_map/dot_general | solution.py:46
  (9 shorter events, 0.1 us)
Async XLA Ops:
  8.0 154.3 %all-reduce.2.cloned.1.call-start = ((), (), s32[]{:S(2)}) async-start(), calls=%async_computation.1 | async-start | bytes 524288 | tf_op jit(solution)/shard_map/psum | solution.py:43
  34.0 149.3 %copy-start = (bf16[16,256]{1,0:T(8,128)(2,1)S(1)}, bf16[16,256]{1,0:T(8,128)(2,1)}, u32[]{:S(2)}) copy-start(bf16[16,256]{1,0:T(8,128)(2,1)} %param.2) | copy-start | bytes 24580
  141.6 41.7 %all-gather.2.cloned.1.call-start = ((), (), s32[]{:S(2)}) async-start(), calls=%async_computation.2 | async-start | bytes 2228224 | tf_op jit(solution)/shard_map/all_gather | solution.py:48
  142.2 11.5 %all-to-all-start = ((bf16[16,16,256]{2,1,0:T(8,128)(2,1)}), bf16[16,16,256]{2,1,0:T(8,128)(2,1)S(1)}, u32[]{:S(2)}, u32[]{:S(2)}) async-start(bf16[16,16,256]{2,1,0:T(8,128)(2,1)} %bitcast.11), calls=%async_computation | async-start | bytes 262144 | tf_op jit(solution)/shard_map/all_to_all | solution.py:45
Sparse Core Ops, SparseCore 0:
  141.7 20.5 all-reduce.1
Sparse Core Ops, SparseCore 1:
  144.4 38.8 all-gather.1
where the time goes:
time: 194 us; the launch traced here: 193 us
  blocking collectives  132 us (68%)
  waiting for transfers between devices  31.5 us (16%)
  between operations  15.5 us (8%)
  matrix products  6.94 us (4%)
  other arithmetic  3.7 us (2%)
  starting transfers between devices  3.6 us (2%)
    psum x3, blocking collectives, shards(): lax.psum(jnp.dot(kernel, weights_cols, precision=lax.Precision.HIGHEST),...  88.6 us
    all_gather x1, blocking collectives, shards(): gathered = lax.all_gather(residuals, 'codes', axis=0, tiled=True)  23.7 us
    all_gather x1, waiting for transfers between devices, shards(): lax.all_gather(codebook, 'codes', axis=0, tiled=True)  19.3 us
    psum x3, blocking collectives, shards(): lax.psum(jnp.dot(weights_rows, kernel, precision=lax.Precision.HIGHEST),...  14.9 us
    psum x1, waiting for transfers between devices, shards(): numerator, mass = lax.psum((numerator, mass), 'items')  8.57 us
    psum x1, blocking collectives, shards(): numerator, mass = lax.psum((numerator, mass), 'items')  4.94 us
  transfers between devices with their start and end apart: 3, of which 3 were waited for; matrix products, arithmetic and copies ran while one was open for 1% of the time, Pallas kernels for 0%

commit v1 on v0

v1 whole, which is shorter than its diff:
```python
import functools
import math

import jax
import jax.numpy as jnp
from jax import lax
from jax.experimental import pallas as pl
from jax.experimental.pallas import tpu as pltpu
from jax.sharding import PartitionSpec as P

ITERS = 3
EPSILON = 1e-06
SHARPNESS = 40.0
PART = jnp.bfloat16
MESH = pl.DeviceIdType.MESH
NT = (((1,), (1,)), ((), ()))
TN = (((0,), (0,)), ((), ()))


def drain(ref, sem):
    pltpu.make_async_copy(ref, ref, sem).wait()


def each(count, body):
    if count <= 32:
        for i in range(count):
            body(i)
    else:
        pl.loop(0, count)(body)


def kernel(
    groups, shards, cores,
    res_ref, code_ref, newc_ref, next_ref,
    items_ref, kern_ref, u_ref, row_out, row_in, part_out, part_in,
    gather_send, gather_recv, pair_send, pair_recv, row_send, row_recv, part_send, part_recv,
):
    f32, bf16 = jnp.float32, jnp.bfloat16
    y, c = lax.axis_index("items"), lax.axis_index("codes")
    rows, features = res_ref.shape
    codes = code_ref.shape[0]
    devices = groups * shards
    items = devices * rows
    line = shards // cores
    half = line * rows
    core, chip = lax.rem(c, cores), lax.div(c, cores)

    def start_of(group, lane):
        return pl.multiple_of((group * cores + lane) * half, half)

    barrier = pltpu.get_barrier_semaphore()
    me = y * shards + c

    def greet(i):
        other = lax.rem(me + i + 1, devices)
        pl.semaphore_signal(
            barrier, inc=1,
            device_id=(lax.div(other, shards), lax.rem(other, shards)), device_id_type=MESH,
        )

    each(devices - 1, greet)

    mine = pl.ds(pl.multiple_of((y * cores + core) * half + chip * rows, rows), rows)
    items_ref[mine, :] = res_ref[...]
    code = code_ref[...]
    code32 = code.astype(f32)
    code_scale = lax.rsqrt(jnp.sum(code32 * code32, axis=1, keepdims=True) / features + EPSILON)
    code_scale = code_scale * (SHARPNESS * math.log2(math.e) / features)
    pl.semaphore_wait(barrier, devices - 1)

    spot = y * line + chip
    chips = groups * line

    def spread(i):
        other = lax.rem(spot + i + 1, chips)
        pltpu.make_async_remote_copy(
            src_ref=res_ref, dst_ref=items_ref.at[mine],
            send_sem=gather_send, recv_sem=gather_recv,
            device_id=(lax.div(other, line), lax.rem(other, line) * cores + core),
            device_id_type=MESH,
        ).start()

    each(chips - 1, spread)
    drain(items_ref.at[pl.ds(0, (chips - 1) * rows)], gather_recv)
    if cores == 2:
        for g in range(groups):
            block = items_ref.at[pl.ds(start_of(g, core), half)]
            pltpu.make_async_remote_copy(
                src_ref=block, dst_ref=block, send_sem=pair_send, recv_sem=pair_recv,
                device_id=(y, c + 1 - 2 * core), device_id_type=MESH,
            ).start()

    ones = jnp.ones((16, features), bf16)

    def build(start):
        block = items_ref[pl.ds(start, half), :]
        sim = lax.dot_general(code, block, NT, preferred_element_type=f32)
        wide = block.astype(f32)
        square = wide * wide
        high = square.astype(bf16)
        low = (square - high.astype(f32)).astype(bf16)
        mean = lax.dot_general(ones, high, NT, preferred_element_type=f32)
        mean = mean + lax.dot_general(ones, low, NT, preferred_element_type=f32)
        row_scale = lax.rsqrt(mean[0:1] / features + EPSILON)
        kern_ref[:, pl.ds(start, half)] = jnp.exp2(sim * code_scale * row_scale)

    each(groups, lambda g: build(start_of(g, core)))
    if cores == 2:
        drain(items_ref.at[pl.ds(0, chips * rows)], pair_recv)
        each(groups, lambda g: build(start_of(g, 1 - core)))

    width = math.gcd(items, 512)
    pieces = items // width

    def lanes(i):
        if pieces == 1:
            return pl.ds(0, width)
        return pl.ds(pl.multiple_of(i * width, width), width)

    def over_pieces(body, carry):
        if pieces == 1:
            return body(0, carry)
        return lax.fori_loop(0, pieces, body, carry)

    balance = items / (codes * shards)

    def column_sum(first):
        def body(i, total):
            k = kern_ref[:, lanes(i)]
            if not first:
                k = k * u_ref[:, lanes(i)]
            return total + jnp.sum(k, axis=1, keepdims=True)
        return over_pieces(body, jnp.zeros((codes, 1), f32))

    def row_sum(sweep, v):
        def body(i, none):
            row_out[sweep, :, lanes(i)] = jnp.sum(kern_ref[:, lanes(i)] * v, axis=0, keepdims=True)
            return none
        over_pieces(body, 0)

    def send_rows(sweep):
        def one(j):
            pltpu.make_async_remote_copy(
                src_ref=row_out.at[sweep], dst_ref=row_in.at[sweep, j],
                send_sem=row_send.at[sweep], recv_sem=row_recv.at[sweep],
                device_id=(y, lax.rem(c + j + 1, shards)), device_id_type=MESH,
            ).start()
        each(shards - 1, one)

    def finish_rows(sweep):
        drain(row_in.at[sweep], row_recv.at[sweep])

        def body(i, none):
            total = row_out[sweep, :, lanes(i)]
            if shards <= 32:
                for j in range(shards - 1):
                    total = total + row_in[sweep, j, :, lanes(i)]
            else:
                total = lax.fori_loop(
                    0, shards - 1, lambda j, t: t + row_in[sweep, j, :, lanes(i)], total
                )
            u_ref[:, lanes(i)] = 1.0 / total
            return none
        over_pieces(body, 0)

    for sweep in range(ITERS):
        v = balance / column_sum(sweep == 0)
        row_sum(sweep, v)
        send_rows(sweep)
        if sweep < ITERS - 1:
            finish_rows(sweep)

    def partial(lane):
        plan = (kern_ref[:, pl.ds(start_of(y, lane), half)] * v).astype(bf16)
        part = lax.dot_general(plan, code, TN, preferred_element_type=f32)
        part_out[pl.ds(lane * half, half), :] = part.astype(part_out.dtype)

    each(cores, partial)

    def send_part(j):
        other = lax.rem(c + j + 1, shards)
        index = lax.rem(other, cores) * line + lax.div(other, cores)
        pltpu.make_async_remote_copy(
            src_ref=part_out.at[pl.ds(pl.multiple_of(index * rows, rows), rows)],
            dst_ref=part_in.at[j],
            send_sem=part_send, recv_sem=part_recv,
            device_id=(y, other), device_id_type=MESH,
        ).start()

    each(shards - 1, send_part)

    finish_rows(ITERS - 1)

    def gather_codes(i, carry):
        numerator, mass = carry
        plan = (kern_ref[:, lanes(i)] * u_ref[:, lanes(i)] * v).astype(bf16)
        block = items_ref[lanes(i), :]
        numerator = numerator + jnp.dot(plan, block, preferred_element_type=f32)
        return numerator, mass + jnp.sum(plan.astype(f32), axis=1, keepdims=True)

    numerator, mass = over_pieces(
        gather_codes, (jnp.zeros((codes, features), f32), jnp.zeros((codes, 1), f32))
    )
    newc_ref[...] = numerator / mass

    start = (y * cores + core) * half + chip * rows
    def pick(i, total):
        lane = lax.broadcasted_iota(jnp.int32, (rows, width), 1) + i * width
        row = lax.broadcasted_iota(jnp.int32, (rows, width), 0) + start
        chosen = jnp.where(lane == row, u_ref[:, lanes(i)], 0.0)
        return total + jnp.sum(chosen, axis=1, keepdims=True)

    u_mine = over_pieces(pick, jnp.zeros((rows, 1), f32))

    drain(part_in, part_recv)
    own = pl.ds(pl.multiple_of((core * line + chip) * rows, rows), rows)
    rebuilt = part_out[own, :].astype(f32)
    if shards <= 32:
        for j in range(shards - 1):
            rebuilt = rebuilt + part_in[j].astype(f32)
    else:
        rebuilt = lax.fori_loop(
            0, shards - 1, lambda j, t: t + part_in[j].astype(f32), rebuilt
        )
    next_ref[...] = res_ref[...].astype(f32) - rebuilt * u_mine

    drain(items_ref.at[pl.ds(0, (chips - 1) * rows)], gather_send)
    if cores == 2:
        drain(items_ref.at[pl.ds(0, chips * rows)], pair_send)
    for sweep in range(ITERS):
        drain(row_in.at[sweep], row_send.at[sweep])
    drain(part_in, part_send)


def shards_of(groups, shards, residuals, codebook):
    rows, features = residuals.shape
    codes = codebook.shape[0]
    cores = 2 if shards % 2 == 0 else 1
    items = groups * shards * rows
    f32, bf16 = jnp.float32, jnp.bfloat16
    dma = pltpu.SemaphoreType.DMA
    vmem = pl.BlockSpec(memory_space=pltpu.VMEM)
    return pl.pallas_call(
        functools.partial(kernel, groups, shards, cores),
        out_shape=(
            jax.ShapeDtypeStruct((codes, features), f32),
            jax.ShapeDtypeStruct((rows, features), f32),
        ),
        in_specs=[vmem, vmem],
        out_specs=(vmem, vmem),
        scratch_shapes=[
            pltpu.VMEM((items, features), bf16),
            pltpu.VMEM((codes, items), f32),
            pltpu.VMEM((1, items), f32),
            pltpu.VMEM((ITERS, 1, items), f32),
            pltpu.VMEM((ITERS, shards - 1, 1, items), f32),
            pltpu.VMEM((shards * rows, features), PART),
            pltpu.VMEM((shards - 1, rows, features), PART),
            dma, dma, dma, dma, dma((ITERS,)), dma((ITERS,)), dma, dma,
        ],
        compiler_params=pltpu.CompilerParams(
            collective_id=0, has_side_effects=True, vmem_limit_bytes=48 * 2**20
        ),
    )(residuals, codebook)


def solution(mesh):
    groups, shards = mesh.shape["items"], mesh.shape["codes"]
    return jax.shard_map(
        functools.partial(shards_of, groups, shards),
        mesh=mesh,
        in_specs=(P(("items", "codes"), None), P("codes", None)),
        out_specs=(P("codes", None), P(("items", "codes"), None)),
        check_vma=False,
    )
```

time: 194 us -> 30.5 us (0.16)
  blocking collectives: 132 us -> 0 us
  waiting for transfers between devices: 31.5 us -> 0 us
  Pallas kernels: 0 us -> 26.7 us
  between operations: 15.5 us -> 0.65 us
  matrix products: 6.94 us -> 0 us
  other arithmetic: 3.7 us -> 0 us
  starting transfers between devices: 3.6 us -> 0 us
  local copies, waits for them, and re-layouts: 0.02 us -> 2.9 us
    psum x7 -> x0, blocking collectives: 108 us -> none  [the longest x3 88.6 us: shards(): lax.psum(jnp.dot(kernel, weights_cols, precision=lax.Precision.HIGHEST),...]
    pallas_call x0 -> x1, Pallas kernels: none -> 26.7 us  [shards_of(): pl.pallas_call(functools.partial(kernel, groups, shards, cores), out_shap...]
    all_gather x1 -> x0, blocking collectives: 23.7 us -> none  [shards(): gathered = lax.all_gather(residuals, 'codes', axis=0, tiled=True)]
    all_gather x1 -> x0, waiting for transfers between devices: 19.3 us -> none  [shards(): lax.all_gather(codebook, 'codes', axis=0, tiled=True)]
    psum x1 -> x0, waiting for transfers between devices: 8.57 us -> none  [shards(): numerator, mass = lax.psum((numerator, mass), 'items')]
    dot_general x9 -> x0, matrix products: 6.94 us -> none  [the longest x1 2.58 us: shards(): jnp.dot(moved, lax.all_gather(codebook, 'codes', axis=0, tiled=True), pre...]
    all_to_all x1 -> x0, starting transfers between devices: 3.52 us -> none  [shards(): lax.all_to_all(transport, 'codes', split_axis=0, concat_axis=1, tiled=True)]
    all_to_all x1 -> x0, waiting for transfers between devices: 3.06 us -> none  [shards(): lax.all_to_all(transport, 'codes', split_axis=0, concat_axis=1, tiled=True)]
  transfers between devices with their start and end apart: 3 -> 0, of which waited for: 3 -> 0; matrix products, arithmetic and copies ran while one was open for 1% -> 0% of each run, Pallas kernels for 0% -> 0%
where the time goes in v1:
time: 30.5 us; the launch traced here: 30.3 us
  Pallas kernels  26.7 us (88%)
  local copies, waits for them, and re-layouts  2.9 us (10%)
  between operations  0.65 us (2%)
    pallas_call x1, Pallas kernels, shards_of(): pl.pallas_call(functools.partial(kernel, groups, shards, cores), out_shap...  26.7 us
    unnamed x6, local copies, waits for them, and re-layouts  2.9 us

profile of v1, /device:TPU:0, one launch (start us, length us, event | category | flops | bytes accessed | tf_op | source)
XLA Modules:
  0.0 30.3 jit_solution(4654619592054352722)
XLA Ops:
  0.6 0.0 copy-start
  0.6 0.9 %copy-done = bf16[256,256]{1,0:T(8,128)(2,1)S(1)} copy-done((bf16[256,256]{1,0:T(8,128)(2,1)S(1)}, bf16[256,256]{1,0:T(8,128)(2,1)}, u32[]{:S(2)}) %copy-start) | copy-done | bytes 131096
  1.5 0.0 copy-start.1
  1.5 0.7 %copy-done.1 = bf16[16,256]{1,0:T(8,128)(2,1)S(1)} copy-done((bf16[16,256]{1,0:T(8,128)(2,1)S(1)}, bf16[16,256]{1,0:T(8,128)(2,1)}, u32[]{:S(2)}) %copy-start.1) | copy-done | bytes 8216
  2.2 26.7 %shard_map.41 = (f32[256,256]{1,0:T(8,128)S(1)}, f32[16,256]{1,0:T(8,128)S(1)}) custom-call(bf16[16,256]{1,0:T(8,128)(2,1)S(1)} %copy-done.1, bf16[256,256]{1,0:T(8,128)(2,1)S(1)} %copy-done), custom_call_target="tpu_custom_call" | custom-call | tf_op jit(solution)/shard_map/pallas_call | solution.py:243
  29.0 0.7 %copy.6 = f32[256,256]{1,0:T(8,128)} copy(f32[256,256]{1,0:T(8,128)S(1)} %get-tuple-element.4) | data formatting | bytes 524288
  29.7 0.6 %copy.7 = f32[16,256]{1,0:T(8,128)} copy(f32[16,256]{1,0:T(8,128)S(1)} %get-tuple-element.5) | data formatting | bytes 32768
Async XLA Ops:
  0.6 0.9 %copy-start = (bf16[256,256]{1,0:T(8,128)(2,1)S(1)}, bf16[256,256]{1,0:T(8,128)(2,1)}, u32[]{:S(2)}) copy-start(bf16[256,256]{1,0:T(8,128)(2,1)} %code_ref.1) | copy-start | bytes 393220
  1.5 0.7 %copy-start.1 = (bf16[16,256]{1,0:T(8,128)(2,1)S(1)}, bf16[16,256]{1,0:T(8,128)(2,1)}, u32[]{:S(2)}) copy-start(bf16[16,256]{1,0:T(8,128)(2,1)} %res_ref.1) | copy-start | bytes 24580

commit v2 on v1

--- a/solution.py
+++ b/solution.py
@@ -31,9 +31,9 @@
 
 def kernel(
     groups, shards, cores,
-    res_ref, code_ref, newc_ref, next_ref,
-    items_ref, kern_ref, u_ref, row_out, row_in, part_out, part_in,
-    gather_send, gather_recv, pair_send, pair_recv, row_send, row_recv, part_send, part_recv,
+    res_hbm, code_hbm, newc_ref, next_ref,
+    res_ref, code_ref, items_ref, kern_ref, u_ref, row_out, row_in, part_out, part_in,
+    load, gather_send, gather_recv, pair_send, pair_recv, row_send, row_recv, part_send, part_recv,
 ):
     f32, bf16 = jnp.float32, jnp.bfloat16
     y, c = lax.axis_index("items"), lax.axis_index("codes")
@@ -49,41 +49,59 @@
         return pl.multiple_of((group * cores + lane) * half, half)
 
     barrier = pltpu.get_barrier_semaphore()
-    me = y * shards + c
-
-    def greet(i):
-        other = lax.rem(me + i + 1, devices)
+    spot = y * line + chip
+    chips = groups * line
+    partners = chips - 1 + (line if cores == 2 else 0)
+
+    def greet_chip(i):
+        other = lax.rem(spot + i + 1, chips)
         pl.semaphore_signal(
             barrier, inc=1,
-            device_id=(lax.div(other, shards), lax.rem(other, shards)), device_id_type=MESH,
+            device_id=(lax.div(other, line), lax.rem(other, line) * cores + core),
+            device_id_type=MESH,
         )
 
-    each(devices - 1, greet)
-
+    def greet_core(i):
+        other = lax.rem(chip + i, line) * cores + 1 - core
+        pl.semaphore_signal(barrier, inc=1, device_id=(y, other), device_id_type=MESH)
+
+    each(chips - 1, greet_chip)
+    if cores == 2:
+        each(line, greet_core)
+    load_res = pltpu.make_async_copy(res_hbm, res_ref, load.at[0])
+    load_code = pltpu.make_async_copy(code_hbm, code_ref, load.at[1])
+    load_res.start()
+    load_code.start()
+
+    load_res.wait()
+    load_code.wait()
     mine = pl.ds(pl.multiple_of((y * cores + core) * half + chip * rows, rows), rows)
     items_ref[mine, :] = res_ref[...]
     code = code_ref[...]
     code32 = code.astype(f32)
     code_scale = lax.rsqrt(jnp.sum(code32 * code32, axis=1, keepdims=True) / features + EPSILON)
     code_scale = code_scale * (SHARPNESS * math.log2(math.e) / features)
-    pl.semaphore_wait(barrier, devices - 1)
-
-    spot = y * line + chip
-    chips = groups * line
+    pl.semaphore_wait(barrier, partners)
 
     def spread(i):
-        other = lax.rem(spot + i + 1, chips)
-        pltpu.make_async_remote_copy(
-            src_ref=res_ref, dst_ref=items_ref.at[mine],
-            send_sem=gather_send, recv_sem=gather_recv,
-            device_id=(lax.div(other, line), lax.rem(other, line) * cores + core),
-            device_id_type=MESH,
-        ).start()
-
-    each(chips - 1, spread)
-    drain(items_ref.at[pl.ds(0, (chips - 1) * rows)], gather_recv)
-    if cores == 2:
-        for g in range(groups):
+        other = lax.rem(2 * chips - 1 - spot - i, chips)
+
+        @pl.when(other != spot)
+        def _():
+            pltpu.make_async_remote_copy(
+                src_ref=res_ref, dst_ref=items_ref.at[mine],
+                send_sem=gather_send, recv_sem=gather_recv.at[y],
+                device_id=(lax.div(other, line), lax.rem(other, line) * cores + core),
+                device_id_type=MESH,
+            ).start()
+
+    each(chips, spread)
+    for i in range(groups):
+        g = lax.rem(y + i, groups)
+        arrive = (line - 1 if i == 0 else line) * rows
+        if arrive:
+            drain(items_ref.at[pl.ds(0, arrive)], gather_recv.at[g])
+        if cores == 2:
             block = items_ref.at[pl.ds(start_of(g, core), half)]
             pltpu.make_async_remote_copy(
                 src_ref=block, dst_ref=block, send_sem=pair_send, recv_sem=pair_recv,
@@ -140,24 +158,29 @@
 
     def send_rows(sweep):
         def one(j):
-            pltpu.make_async_remote_copy(
-                src_ref=row_out.at[sweep], dst_ref=row_in.at[sweep, j],
-                send_sem=row_send.at[sweep], recv_sem=row_recv.at[sweep],
-                device_id=(y, lax.rem(c + j + 1, shards)), device_id_type=MESH,
-            ).start()
-        each(shards - 1, one)
+            other = lax.rem(2 * shards - 1 - c - j, shards)
+
+            @pl.when(other != c)
+            def _():
+                pltpu.make_async_remote_copy(
+                    src_ref=row_out.at[sweep], dst_ref=row_in.at[sweep, c],
+                    send_sem=row_send.at[sweep], recv_sem=row_recv.at[sweep],
+                    device_id=(y, other), device_id_type=MESH,
+                ).start()
+        each(shards, one)
 
     def finish_rows(sweep):
-        drain(row_in.at[sweep], row_recv.at[sweep])
+        drain(row_in.at[sweep, pl.ds(0, shards - 1)], row_recv.at[sweep])
+        row_in[sweep, c] = row_out[sweep]
 
         def body(i, none):
-            total = row_out[sweep, :, lanes(i)]
+            total = jnp.zeros((1, width), f32)
             if shards <= 32:
-                for j in range(shards - 1):
+                for j in range(shards):
                     total = total + row_in[sweep, j, :, lanes(i)]
             else:
                 total = lax.fori_loop(
-                    0, shards - 1, lambda j, t: t + row_in[sweep, j, :, lanes(i)], total
+                    0, shards, lambda j, t: t + row_in[sweep, j, :, lanes(i)], total
                 )
             u_ref[:, lanes(i)] = 1.0 / total
             return none
@@ -178,16 +201,19 @@
     each(cores, partial)
 
     def send_part(j):
-        other = lax.rem(c + j + 1, shards)
+        other = lax.rem(2 * shards - 1 - c - j, shards)
         index = lax.rem(other, cores) * line + lax.div(other, cores)
-        pltpu.make_async_remote_copy(
-            src_ref=part_out.at[pl.ds(pl.multiple_of(index * rows, rows), rows)],
-            dst_ref=part_in.at[j],
-            send_sem=part_send, recv_sem=part_recv,
-            device_id=(y, other), device_id_type=MESH,
-        ).start()
-
-    each(shards - 1, send_part)
+
+        @pl.when(other != c)
+        def _():
+            pltpu.make_async_remote_copy(
+                src_ref=part_out.at[pl.ds(pl.multiple_of(index * rows, rows), rows)],
+                dst_ref=part_in.at[c],
+                send_sem=part_send, recv_sem=part_recv,
+                device_id=(y, other), device_id_type=MESH,
+            ).start()
+
+    each(shards, send_part)
 
     finish_rows(ITERS - 1)
 
@@ -212,15 +238,16 @@
 
     u_mine = over_pieces(pick, jnp.zeros((rows, 1), f32))
 
-    drain(part_in, part_recv)
+    drain(part_in.at[pl.ds(0, shards - 1)], part_recv)
     own = pl.ds(pl.multiple_of((core * line + chip) * rows, rows), rows)
-    rebuilt = part_out[own, :].astype(f32)
+    part_in[c] = part_out[own, :]
+    rebuilt = jnp.zeros((rows, features), f32)
     if shards <= 32:
-        for j in range(shards - 1):
+        for j in range(shards):
             rebuilt = rebuilt + part_in[j].astype(f32)
     else:
         rebuilt = lax.fori_loop(
-            0, shards - 1, lambda j, t: t + part_in[j].astype(f32), rebuilt
+            0, shards, lambda j, t: t + part_in[j].astype(f32), rebuilt
         )
     next_ref[...] = res_ref[...].astype(f32) - rebuilt * u_mine
 
@@ -228,8 +255,8 @@
     if cores == 2:
         drain(items_ref.at[pl.ds(0, chips * rows)], pair_send)
     for sweep in range(ITERS):
-        drain(row_in.at[sweep], row_send.at[sweep])
-    drain(part_in, part_send)
+        drain(row_in.at[sweep, pl.ds(0, shards - 1)], row_send.at[sweep])
+    drain(part_in.at[pl.ds(0, shards - 1)], part_send)
 
 
 def shards_of(groups, shards, residuals, codebook):
@@ -240,23 +267,26 @@
     f32, bf16 = jnp.float32, jnp.bfloat16
     dma = pltpu.SemaphoreType.DMA
     vmem = pl.BlockSpec(memory_space=pltpu.VMEM)
+    hbm = pl.BlockSpec(memory_space=pltpu.HBM)
     return pl.pallas_call(
         functools.partial(kernel, groups, shards, cores),
         out_shape=(
             jax.ShapeDtypeStruct((codes, features), f32),
             jax.ShapeDtypeStruct((rows, features), f32),
         ),
-        in_specs=[vmem, vmem],
+        in_specs=[hbm, hbm],
         out_specs=(vmem, vmem),
         scratch_shapes=[
+            pltpu.VMEM((rows, features), bf16),
+            pltpu.VMEM((codes, features), bf16),
             pltpu.VMEM((items, features), bf16),
             pltpu.VMEM((codes, items), f32),
             pltpu.VMEM((1, items), f32),
             pltpu.VMEM((ITERS, 1, items), f32),
-            pltpu.VMEM((ITERS, shards - 1, 1, items), f32),
+            pltpu.VMEM((ITERS, shards, 1, items), f32),
             pltpu.VMEM((shards * rows, features), PART),
-            pltpu.VMEM((shards - 1, rows, features), PART),
-            dma, dma, dma, dma, dma((ITERS,)), dma((ITERS,)), dma, dma,
+            pltpu.VMEM((shards, rows, features), PART),
+            dma((2,)), dma, dma((groups,)), dma, dma, dma((ITERS,)), dma((ITERS,)), dma, dma,
         ],
         compiler_params=pltpu.CompilerParams(
             collective_id=0, has_side_effects=True, vmem_limit_bytes=48 * 2**20

time: 30.5 us -> 30.3 us (level)
  no operation moved by 1% of the time
where the time goes in v2:
time: 30.3 us; the launch traced here: 30.1 us
  Pallas kernels  26.5 us (87%)
  local copies, waits for them, and re-layouts  2.9 us (10%)
  between operations  0.65 us (2%)
    pallas_call x1, Pallas kernels, shards_of(): pl.pallas_call(functools.partial(kernel, groups, shards, cores), out_shap...  26.5 us
    unnamed x6, local copies, waits for them, and re-layouts  2.9 us

profile of v2, /device:TPU:0, one launch (start us, length us, event | category | flops | bytes accessed | tf_op | source)
XLA Modules:
  0.0 30.1 jit_solution(2916078675807915836)
XLA Ops:
  0.6 0.0 copy-start
  0.6 0.9 %copy-done = bf16[256,256]{1,0:T(8,128)(2,1)S(1)} copy-done((bf16[256,256]{1,0:T(8,128)(2,1)S(1)}, bf16[256,256]{1,0:T(8,128)(2,1)}, u32[]{:S(2)}) %copy-start) | copy-done | bytes 131096
  1.5 0.0 copy-start.1
  1.5 0.7 %copy-done.1 = bf16[16,256]{1,0:T(8,128)(2,1)S(1)} copy-done((bf16[16,256]{1,0:T(8,128)(2,1)S(1)}, bf16[16,256]{1,0:T(8,128)(2,1)}, u32[]{:S(2)}) %copy-start.1) | copy-done | bytes 8216
  2.2 26.5 %shard_map.41 = (f32[256,256]{1,0:T(8,128)S(1)}, f32[16,256]{1,0:T(8,128)S(1)}) custom-call(bf16[16,256]{1,0:T(8,128)(2,1)S(1)} %copy-done.1, bf16[256,256]{1,0:T(8,128)(2,1)S(1)} %copy-done), custom_call_target="tpu_custom_call" | custom-call | tf_op jit(solution)/shard_map/pallas_call | solution.py:271
  28.8 0.7 %copy.6 = f32[256,256]{1,0:T(8,128)} copy(f32[256,256]{1,0:T(8,128)S(1)} %get-tuple-element.4) | data formatting | bytes 524288
  29.5 0.6 %copy.7 = f32[16,256]{1,0:T(8,128)} copy(f32[16,256]{1,0:T(8,128)S(1)} %get-tuple-element.5) | data formatting | bytes 32768
Async XLA Ops:
  0.6 0.9 %copy-start = (bf16[256,256]{1,0:T(8,128)(2,1)S(1)}, bf16[256,256]{1,0:T(8,128)(2,1)}, u32[]{:S(2)}) copy-start(bf16[256,256]{1,0:T(8,128)(2,1)} %code_hbm.1) | copy-start | bytes 393220
  1.5 0.7 %copy-start.1 = (bf16[16,256]{1,0:T(8,128)(2,1)S(1)}, bf16[16,256]{1,0:T(8,128)(2,1)}, u32[]{:S(2)}) copy-start(bf16[16,256]{1,0:T(8,128)(2,1)} %res_hbm.1) | copy-start | bytes 24580

commit v3 on v2

--- a/solution.py
+++ b/solution.py
@@ -193,33 +193,39 @@
         if sweep < ITERS - 1:
             finish_rows(sweep)
 
+    def scale(i, none):
+        kern_ref[:, lanes(i)] = kern_ref[:, lanes(i)] * v
+        return none
+
+    over_pieces(scale, 0)
+
     def partial(lane):
-        plan = (kern_ref[:, pl.ds(start_of(y, lane), half)] * v).astype(bf16)
+        plan = kern_ref[:, pl.ds(start_of(y, lane), half)].astype(bf16)
         part = lax.dot_general(plan, code, TN, preferred_element_type=f32)
         part_out[pl.ds(lane * half, half), :] = part.astype(part_out.dtype)
 
-    each(cores, partial)
-
-    def send_part(j):
-        other = lax.rem(2 * shards - 1 - c - j, shards)
-        index = lax.rem(other, cores) * line + lax.div(other, cores)
+    def send_part(lane, i):
+        place = lax.rem(2 * line - 1 - chip - i, line)
+        other = place * cores + lane
 
         @pl.when(other != c)
         def _():
             pltpu.make_async_remote_copy(
-                src_ref=part_out.at[pl.ds(pl.multiple_of(index * rows, rows), rows)],
+                src_ref=part_out.at[pl.ds(pl.multiple_of((lane * line + place) * rows, rows), rows)],
                 dst_ref=part_in.at[c],
                 send_sem=part_send, recv_sem=part_recv,
                 device_id=(y, other), device_id_type=MESH,
             ).start()
 
-    each(shards, send_part)
+    for lane in range(cores):
+        partial(lane)
+        each(line, functools.partial(send_part, lane))
 
     finish_rows(ITERS - 1)
 
     def gather_codes(i, carry):
         numerator, mass = carry
-        plan = (kern_ref[:, lanes(i)] * u_ref[:, lanes(i)] * v).astype(bf16)
+        plan = (kern_ref[:, lanes(i)] * u_ref[:, lanes(i)]).astype(bf16)
         block = items_ref[lanes(i), :]
         numerator = numerator + jnp.dot(plan, block, preferred_element_type=f32)
         return numerator, mass + jnp.sum(plan.astype(f32), axis=1, keepdims=True)

time: 30.3 us -> 30.2 us (level)
  the two profiles are of different devices: /device:TPU:0 before, /device:TPU:1 now
where the time goes in v3:
time: 30.2 us; the launch traced here: 30 us
  Pallas kernels  26.4 us (87%)
  local copies, waits for them, and re-layouts  2.9 us (10%)
  between operations  0.65 us (2%)
    pallas_call x1, Pallas kernels, shards_of(): pl.pallas_call(functools.partial(kernel, groups, shards, cores), out_shap...  26.4 us
    unnamed x6, local copies, waits for them, and re-layouts  2.9 us

profile of v3, /device:TPU:1, one launch (start us, length us, event | category | flops | bytes accessed | tf_op | source)
XLA Modules:
  0.0 30.0 jit_solution(11110901690138648732)
XLA Ops:
  0.6 0.0 copy-start
  0.6 0.9 %copy-done = bf16[256,256]{1,0:T(8,128)(2,1)S(1)} copy-done((bf16[256,256]{1,0:T(8,128)(2,1)S(1)}, bf16[256,256]{1,0:T(8,128)(2,1)}, u32[]{:S(2)}) %copy-start) | copy-done | bytes 131096
  1.5 0.0 copy-start.1
  1.5 0.7 %copy-done.1 = bf16[16,256]{1,0:T(8,128)(2,1)S(1)} copy-done((bf16[16,256]{1,0:T(8,128)(2,1)S(1)}, bf16[16,256]{1,0:T(8,128)(2,1)}, u32[]{:S(2)}) %copy-start.1) | copy-done | bytes 8216
  2.2 26.4 %shard_map.41 = (f32[256,256]{1,0:T(8,128)S(1)}, f32[16,256]{1,0:T(8,128)S(1)}) custom-call(bf16[16,256]{1,0:T(8,128)(2,1)S(1)} %copy-done.1, bf16[256,256]{1,0:T(8,128)(2,1)S(1)} %copy-done), custom_call_target="tpu_custom_call" | custom-call | tf_op jit(solution)/shard_map/pallas_call | solution.py:277
  28.6 0.7 %copy.6 = f32[256,256]{1,0:T(8,128)} copy(f32[256,256]{1,0:T(8,128)S(1)} %get-tuple-element.4) | data formatting | bytes 524288
  29.4 0.6 %copy.7 = f32[16,256]{1,0:T(8,128)} copy(f32[16,256]{1,0:T(8,128)S(1)} %get-tuple-element.5) | data formatting | bytes 32768
Async XLA Ops:
  0.6 0.9 %copy-start = (bf16[256,256]{1,0:T(8,128)(2,1)S(1)}, bf16[256,256]{1,0:T(8,128)(2,1)}, u32[]{:S(2)}) copy-start(bf16[256,256]{1,0:T(8,128)(2,1)} %code_hbm.1) | copy-start | bytes 393220
  1.5 0.7 %copy-start.1 = (bf16[16,256]{1,0:T(8,128)(2,1)S(1)}, bf16[16,256]{1,0:T(8,128)(2,1)}, u32[]{:S(2)}) copy-start(bf16[16,256]{1,0:T(8,128)(2,1)} %res_hbm.1) | copy-start | bytes 24580
